TPU v7x, 32 devices: a whole 2x2x4 slice. The times are simulated.
32 devices in a mesh: ens: 4 (over z), rep: 8 (over y, x, core).
Axes of the slice: x: 2, y: 2, z: 4, core: 2. Of those that a mesh axis runs over, the one named last changes fastest.
Arguments:
- cur_states: bfloat16 [8192, 4096], P('rep'), may hold values from -6 to 6
- buffer: bfloat16 [2048, 4096], P('rep'), may hold values from -6 to 6
- fetch_rows: int32 [8, 8, 128], P('rep'), may hold values from 0 to 255
- fetch_counts: int32 [8, 8], replicated, may hold values from 1 to 128, as said below
- actions: int32 [8192], P('rep'), may hold values from 0 to 255
- rewards: float32 [8192], P('rep'), may hold values from -0.5 to 0.5
- terminal: int32 [8192], P('rep'), may hold values 0 or 1
- mc_return: float32 [8192], P('rep'), may hold values from 0 to 1
- w_in: bfloat16 [4, 4096, 512], P('ens'), may hold values from -0.09375 to 0.09375
- w_out: bfloat16 [4, 512, 256], P('ens'), may hold values from -0.25 to 0.25
Outputs:
- targets: float32 [8192], P('rep')
- grad_in: float32 [4, 4096, 512], P('ens', 'rep')
- grad_out: float32 [4, 512, 256], P('ens', 'rep')
Inputs may be any that keep to these rules, and one draw needn't show every extreme that they name: `fetch_rows`: each entry indexes the owner's own rows. `fetch_counts`: entry [o, r] is how many leading slots of requester r at owner o are used; some entry equals 128 in every draw.
All inputs are finite; a program needn't handle non-finite values. No bound on the sum of `terminal` on one device may be relied on, other than what follows from the above.
Results may differ from a plain program's by a relative error of at most 0.0044.
Values may be sent and summed in bfloat16 or wider, within the bound.
A program may use at most 192 MiB of HBM per device.

v0:
```python
import jax
import jax.numpy as jnp
from jax import lax
from jax.sharding import PartitionSpec as P


def critic_head(features, w_first, w_second):
    preact = jnp.dot(features, w_first, preferred_element_type=jnp.float32)
    sigmoid_pre = jax.nn.sigmoid(preact)
    hidden = (preact * sigmoid_pre).astype(jnp.bfloat16)
    values = jax.nn.sigmoid(jnp.dot(hidden, w_second, preferred_element_type=jnp.float32))
    return (preact, sigmoid_pre, hidden, values)


def shards(
    cur_states, buffer, fetch_rows, fetch_counts, actions, rewards, terminal, mc_return, w_in, w_out
):
    my_index = lax.axis_index("rep")
    owners = lax.axis_size("rep")
    slots_per = fetch_rows.shape[2]
    width = buffer.shape[1]
    w_first = w_in[0]
    w_second = w_out[0]
    my_counts = lax.dynamic_slice_in_dim(fetch_counts, my_index, 1, 1)[:, 0]
    slot_ids = jnp.arange(slots_per, dtype=jnp.int32)
    used = (slot_ids[None, :] < my_counts[:, None]).reshape(-1).astype(jnp.float32)
    counted = jnp.sum(fetch_counts).astype(jnp.float32)
    picked = jnp.take(buffer, fetch_rows[0].reshape(-1), axis=0).reshape(owners, slots_per, width)
    values = critic_head(picked.reshape(-1, width), w_first, w_second)[3]
    served = jnp.max(values, axis=1).reshape(picked.shape[0], picked.shape[1])
    best_next = lax.all_to_all(served, "rep", split_axis=0, concat_axis=0, tiled=True).reshape(-1)
    ens_floor = lax.pmin(best_next, "ens")
    bootstrap = jnp.maximum(ens_floor, mc_return)
    target = rewards + 0.98 * (1.0 - terminal.astype(jnp.float32)) * bootstrap
    targets = used * target
    chosen = actions[:, None] == jnp.arange(w_second.shape[1], dtype=jnp.int32)[None, :]
    preact, sigmoid_pre, hidden, values = critic_head(cur_states, w_first, w_second)
    taken = jnp.sum(jnp.where(chosen, values, 0.0), axis=1)
    errors = used * 2.0 * (taken - target) * taken * (1.0 - taken) * (65536.0 / counted)
    d_logits = jnp.where(chosen, errors[:, None], 0.0).astype(jnp.bfloat16)
    grad_second = lax.dot_general(
        hidden, d_logits, (((0,), (0,)), ((), ())), preferred_element_type=jnp.float32
    )
    back = lax.dot_general(
        d_logits, w_second, (((1,), (1,)), ((), ())), preferred_element_type=jnp.float32
    )
    d_hidden = (back * sigmoid_pre * (1.0 + preact * (1.0 - sigmoid_pre))).astype(jnp.bfloat16)
    grad_first = lax.dot_general(
        cur_states, d_hidden, (((0,), (0,)), ((), ())), preferred_element_type=jnp.float32
    )
    share_first, share_second = (
        lax.psum_scatter(grad_first, "rep", scatter_dimension=0, tiled=True),
        lax.psum_scatter(grad_second, "rep", scatter_dimension=0, tiled=True),
    )
    return (targets, share_first[None], share_second[None])


def solution(mesh):
    placed = (
        P("rep", None),
        P("rep", None),
        P("rep", None, None),
        P(),
        P("rep"),
        P("rep"),
        P("rep"),
        P("rep"),
        P("ens", None, None),
        P("ens", None, None),
    )
    return jax.shard_map(
        shards,
        mesh=mesh,
        in_specs=placed,
        out_specs=(P("rep"), P("ens", "rep", None), P("ens", "rep", None)),
        check_vma=False,
    )
```

profile of v0, /device:TPU:0, one launch (start us, length us, event | category | flops | bytes accessed | tf_op | source)
XLA Modules:
  0.0 183.4 jit_solution(3453467498333396282)
XLA Ops:
  7.2 0.0 copy-start
  7.2 0.8 compare_and_fusion
  8.0 0.7 compare_select_fusion
  8.7 0.1 copy-done
  8.8 0.0 copy-start.5
  8.8 7.7 %gather_fusion = bf16[1024,4096]{1,0:T(8,128)(2,1)} fusion(bf16[256,4096]{1,0:T(8,128)(2,1)S(1)} %copy-done, s32[1024]{0:T(1024)S(1)} %broadcast_clamp_fusion), kind=kCustom, calls=%fused_computation | custom fusion | bytes 16781312 | tf_op jit(solution)/shard_map/jit(_take)/gather | solution.py:28
  16.5 0.0 copy-done.5
  16.5 10.4 %fusion.14 = f32[1024]{0:T(1024)} fusion(bf16[1024,4096]{1,0:T(8,128)(2,1)} %gather_fusion, pred[1024]{0:T(1024)(128)(4,1)S(1)} %compare_and_fusion, bf16[1,4096,512]{2,1,0:T(8,128)(2,1)} %param.18, bf16[1,512,256]{2,1,0:T(8,128)(2,1)S(1)} %copy-done.5), kind=kOutput, calls=%fused_computation.22 | convolution fusion | flops 4571266048 | bytes 12850176 | tf_op jit(solution)/shard_map/dot_general | solution.py:11
  26.9 5.2 %all-to-all-start = ((f32[8,1,128]{2,1,0:T(1,128)}), f32[8,1,128]{2,1,0:T(1,128)S(1)}, u32[]{:S(2)}, u32[]{:S(2)}) async-start(f32[8,1,128]{2,1,0:T(1,128)} %bitcast.6), calls=%async_computation | async-start | bytes 8192 | tf_op jit(solution)/shard_map/all_to_all | solution.py:31
  32.1 0.0 copy-start.6
  32.1 0.0 reduce-scatter.3.cloned.1.call-start
  32.1 10.7 %multiply_convert_fusion.1 = (bf16[1024,512]{1,0:T(8,128)(2,1)S(1)}, f32[1024,512]{1,0:T(8,128)}) fusion(bf16[1024,4096]{1,0:T(8,128)(2,1)} %param.10, bf16[1,4096,512]{2,1,0:T(8,128)(2,1)} %param.18), kind=kOutput, calls=%fused_computation.10 | convolution fusion | flops 4297588736 | bytes 15728640 | tf_op jit(solution)/shard_map/dot_general | solution.py:8
  42.8 0.0 copy-done.6
  42.8 0.0 copy-start.1
  42.8 0.0 copy-start.2
  42.8 0.0 copy-start.3
  42.8 0.0 copy-start.4
  42.8 0.6 fusion.15
  43.5 0.0 copy-done.1
  43.5 0.6 reduce_sum.19
  44.1 0.2 dynamic-slice_reduce_fusion
  45.0 0.0 all-to-all-done
  45.0 12.0 %pmin.7 = f32[1024]{0:T(1024)S(1)} all-reduce(f32[1024]{0:T(1024)S(1)} %bitcast.43), channel_id=1, replica_groups=mesh['ens'=4,'rep'=8] {'ens'}, use_global_device_ids=true, to_apply=%region_1.2 | all-reduce | flops 1024 | bytes 8192 | tf_op jit(solution)/shard_map/pmin | solution.py:32
  57.0 0.0 copy-done.2
  57.0 0.0 copy-done.3
  57.0 0.0 copy-done.4
  57.0 0.1 multiply_multiply_fusion
  57.1 11.2 %convolution_bitcast_fusion = f32[4096,512]{0,1:T(8,128)} fusion(bf16[1024,4096]{1,0:T(8,128)(2,1)} %param.10, f32[1024,512]{1,0:T(8,128)} %get-tuple-element.9, bf16[1024]{0:T(1024)(128)(2,1)S(1)} %get-tuple-element.6, s32[1024]{0:T(1024)S(1)} %copy-done.6, bf16[1,512,256]{2,1,0:T(8,128)(2,1)S(1)} %copy-done.5), kind=kOutput, calls=%fused_computation.4 | convolution fusion | flops 4568645632 | bytes 19142656 | tf_op jit(solution)/shard_map/dot_general | solution.py:48
  68.3 0.0 reduce-scatter.3.cloned.1.call-update
  68.3 0.0 reduce-scatter.5.cloned.1.call-start
  68.4 1.3 fusion.25
  69.7 0.0 reduce-scatter.5.cloned.1.call-update
  69.7 0.7 fusion.40
  70.4 68.1 %reduce-scatter.3.cloned.1.call-done = f32[512,512]{0,1:T(8,128)} async-done(((f32[4096,512]{0,1:T(8,128)}), f32[512,512]{0,1:T(8,128)}) %reduce-scatter.3.cloned.1.call-update) | async-done | bytes 1048592 | tf_op jit(solution)/shard_map/reduce_scatter | solution.py:52
  138.4 2.5 %copy.13 = f32[1,512,512]{2,1,0:T(8,128)} copy(f32[1,512,512]{1,2,0:T(8,128)} %bitcast.41) | data formatting | bytes 2097152
  141.0 35.6 %reduce-scatter.5.cloned.1.call-done = f32[64,256]{1,0:T(8,128)} async-done(((f32[512,256]{1,0:T(8,128)}), f32[64,256]{1,0:T(8,128)}) %reduce-scatter.5.cloned.1.call-update) | async-done | bytes 65552 | tf_op jit(solution)/shard_map/reduce_scatter | solution.py:53
  (1 shorter events, 0.0 us)
Async XLA Ops:
  7.2 1.6 copy-start
  8.8 7.7 %copy-start.5 = (bf16[1,512,256]{2,1,0:T(8,128)(2,1)S(1)}, bf16[1,512,256]{2,1,0:T(8,128)(2,1)}, u32[]{:S(2)}) copy-start(bf16[1,512,256]{2,1,0:T(8,128)(2,1)} %param.19) | copy-start | bytes 786436
  26.9 18.1 %all-to-all-start = ((f32[8,1,128]{2,1,0:T(1,128)}), f32[8,1,128]{2,1,0:T(1,128)S(1)}, u32[]{:S(2)}, u32[]{:S(2)}) async-start(f32[8,1,128]{2,1,0:T(1,128)} %bitcast.6), calls=%async_computation | async-start | bytes 8192 | tf_op jit(solution)/shard_map/all_to_all | solution.py:31
  32.1 10.7 %copy-start.6 = (s32[1024]{0:T(1024)S(1)}, s32[1024]{0:T(1024)}, u32[]{:S(2)}) copy-start(s32[1024]{0:T(1024)} %param.14) | copy-start | bytes 12292
  32.1 106.4 %reduce-scatter.3.cloned.1.call-start = ((), (), s32[]{:S(2)}) async-start(), calls=%async_computation.3 | async-start | bytes 9437184 | tf_op jit(solution)/shard_map/reduce_scatter | solution.py:52
  42.8 0.7 copy-start.1
  42.8 14.2 %copy-start.2 = (f32[1024]{0:T(1024)S(1)}, f32[1024]{0:T(1024)}, u32[]{:S(2)}) copy-start(f32[1024]{0:T(1024)} %param.15) | copy-start | bytes 12292
  42.8 14.2 %copy-start.3 = (f32[1024]{0:T(1024)S(1)}, f32[1024]{0:T(1024)}, u32[]{:S(2)}) copy-start(f32[1024]{0:T(1024)} %param.17) | copy-start | bytes 12292
  42.8 14.2 %copy-start.4 = (s32[1024]{0:T(1024)S(1)}, s32[1024]{0:T(1024)}, u32[]{:S(2)}) copy-start(s32[1024]{0:T(1024)} %param.16) | copy-start | bytes 12292
  68.3 108.2 %reduce-scatter.5.cloned.1.call-start = ((), (), s32[]{:S(2)}) async-start(), calls=%async_computation.4 | async-start | bytes 589824 | tf_op jit(solution)/shard_map/reduce_scatter | solution.py:53
Sparse Core Ops, SparseCore 0:
  68.5 69.9 reduce-scatter.2
  142.4 34.0 reduce-scatter.4
where the time goes:
time: 184 us; the launch traced here: 183 us
  waiting for transfers between devices  104 us (57%)
  matrix products  34.2 us (19%)
  between operations  14.8 us (8%)
  blocking collectives  12 us (7%)
  local copies, waits for them, and re-layouts  10.5 us (6%)
  starting transfers between devices  5.26 us (3%)
  other arithmetic  2.92 us (2%)
    reduce_scatter x1, waiting for transfers between devices, shards(): lax.psum_scatter(grad_first, 'rep', scatter_dimension=0, tiled=True)  68.1 us
    reduce_scatter x1, waiting for transfers between devices, shards(): lax.psum_scatter(grad_second, 'rep', scatter_dimension=0, tiled=True)  35.6 us
    pmin x1, blocking collectives, shards(): ens_floor = lax.pmin(best_next, 'ens')  12 us
    dot_general x1, matrix products, shards(): lax.dot_general(cur_states, d_hidden, (((0,), (0,)), ((), ())), preferred...  11.2 us
    dot_general x2, matrix products, critic_head(): jnp.dot(hidden, w_second, preferred_element_type=jnp.float32)  11 us
    dot_general x1, matrix products, critic_head(): preact = jnp.dot(features, w_first, preferred_element_type=jnp.float32)  10.7 us
    gather x1, local copies, waits for them, and re-layouts, shards(): jnp.take(buffer, fetch_rows[0].reshape(-1), axis=0)  7.73 us
    all_to_all x1, starting transfers between devices, shards(): lax.all_to_all(served, 'rep', split_axis=0, concat_axis=0, tiled=True)  5.17 us
  transfers between devices with their start and end apart: 3, of which 2 were waited for; matrix products, arithmetic and copies ran while one was open for 9% of the time, Pallas kernels for 0%

commit v1 on v0

v1 whole, which is shorter than its diff:
```python
import functools

import jax
import jax.numpy as jnp
from jax import lax
from jax.experimental import pallas as pl
from jax.experimental.pallas import tpu as pltpu
from jax.sharding import PartitionSpec as P

F32 = jnp.float32
BF16 = jnp.bfloat16
MESH = pl.DeviceIdType.MESH


def flip(value, bits, size):
    out, base = 0, 1
    while base < size:
        out = out + ((value // base + (bits // base) % 2) % 2) * base
        base *= 2
    return out


def kernel(
    n, members, tile,
    cur_hbm, buf_hbm, fetch_ref, counts_ref, act_ref, rew_ref, term_ref, mc_ref, win_hbm, wout_ref,
    tgt_ref, gin_ref, gout_ref,
    cur, buf, win, wout_t, hid, slope_t, tk, dh_t, gout, mine, ens_got, serve, got,
    own, core_src, core_got, chip_src, chip_got,
    in_sem, cur_sem, ens_ss, ens_rs, rep_ss, rep_rs, core_ss, core_rs, chip_ss, chip_rs,
):
    me, member = lax.axis_index("rep"), lax.axis_index("ens")
    slots, width = cur.shape
    head, bins = wout_ref.shape
    cap = fetch_ref.shape[1]
    rows = buf.shape[0]
    tiles = slots // tile
    chips = n // 2
    chip, core = me // 2, me % 2
    share = width // n
    side = share // bins
    half = head // n // side

    load_win = pltpu.make_async_copy(win_hbm, win, in_sem.at[0])
    load_buf = pltpu.make_async_copy(buf_hbm, buf, in_sem.at[1])
    load_win.start()
    load_buf.start()

    def load_cur(i):
        part = pl.ds(pl.multiple_of(i * tile, tile), tile)
        return pltpu.make_async_copy(cur_hbm.at[part], cur.at[part], cur_sem.at[i])

    for i in range(tiles):
        load_cur(i).start()

    barrier = pltpu.get_barrier_semaphore()
    for d in range(1, members):
        pl.semaphore_signal(barrier, inc=1, device_id={"ens": (member + d) % members}, device_id_type=MESH)
    for d in range(1, n):
        pl.semaphore_signal(barrier, inc=1, device_id={"rep": (me + d) % n}, device_id_type=MESH)

    wout_t[...] = wout_ref[...].astype(F32).T.astype(BF16)
    counted = jnp.int32(0)
    for a in range(n):
        for b in range(n):
            counted = counted + counts_ref[a, b]
    gain = 65536.0 / jnp.full((1, cap), counted, jnp.int32).astype(F32)

    def logits_of(hidden):
        return lax.dot_general(
            wout_t[...], hidden, (((1,), (1,)), ((), ())), preferred_element_type=F32
        )

    load_win.wait()
    load_buf.wait()
    pre = jnp.dot(buf[...], win[...], preferred_element_type=F32)
    hidden = (pre * jax.nn.sigmoid(pre)).astype(BF16)
    best = jnp.max(logits_of(hidden), axis=0, keepdims=True)
    mine[...] = jnp.broadcast_to(best, mine.shape)
    pl.semaphore_wait(barrier, members - 1 + n - 1)

    def ens_copy(d):
        return pltpu.make_async_remote_copy(
            src_ref=mine, dst_ref=ens_got.at[d - 1], send_sem=ens_ss.at[d - 1], recv_sem=ens_rs.at[d - 1],
            device_id={"ens": (member + d) % members}, device_id_type=MESH,
        )

    for d in range(1, members):
        ens_copy(d).start()

    def forward(i, carry):
        load_cur(i).wait()
        part = pl.ds(pl.multiple_of(i * tile, tile), tile)
        pre = jnp.dot(cur[part, :], win[...], preferred_element_type=F32)
        sig = jax.nn.sigmoid(pre)
        hidden = (pre * sig).astype(BF16)
        hid[part, :] = hidden
        slope_t[:, part] = (sig * (1.0 + pre * (1.0 - sig))).T
        logits = logits_of(hidden)
        chosen = lax.broadcasted_iota(jnp.int32, (bins, tile), 0) == act_ref[0:1, part]
        tk[0:1, part] = jnp.sum(jnp.where(chosen, logits, 0.0), axis=0, keepdims=True)
        return carry

    lax.fori_loop(0, tiles // 2, forward, 0)

    floor = mine[0:1, :]
    for d in range(1, members):
        ens_copy(d).wait()
        floor = jnp.minimum(floor, ens_got[d - 1, 0:1, :])
    eye = lax.broadcasted_iota(jnp.int32, (rows, rows), 0) == lax.broadcasted_iota(jnp.int32, (rows, rows), 1)
    floor_col = jnp.sum(jnp.where(eye, jnp.broadcast_to(floor, (rows, rows)), 0.0), axis=1, keepdims=True)
    row_ids = lax.broadcasted_iota(jnp.int32, (rows, cap), 0)
    for r in range(n):
        hit = row_ids == fetch_ref[r:r + 1, :]
        served = jnp.sum(jnp.where(hit, jnp.broadcast_to(floor_col, (rows, cap)), 0.0), axis=0, keepdims=True)
        serve[r] = jnp.broadcast_to(served, serve.shape[1:])

    def rep_copy(d, slot):
        dst = (me + d) % n
        return pltpu.make_async_remote_copy(
            src_ref=serve.at[dst], dst_ref=got.at[slot], send_sem=rep_ss.at[d - 1], recv_sem=rep_rs.at[slot],
            device_id={"rep": dst}, device_id_type=MESH,
        )

    for d in range(1, n):
        rep_copy(d, me).start()
    got[me] = serve[me]

    lax.fori_loop(tiles // 2, tiles, forward, 0)

    for d in range(1, n):
        rep_copy(d, (me + n - d) % n).wait_recv()
    place = lax.broadcasted_iota(jnp.int32, (1, cap), 1)
    bin_ids = lax.broadcasted_iota(jnp.int32, (bins, cap), 0)
    pieces = []
    for o in range(n):
        part = slice(o * cap, (o + 1) * cap)
        used = jnp.where(place < counts_ref[o, me], 1.0, 0.0)
        bootstrap = jnp.maximum(jax.nn.sigmoid(got[o, 0:1, :]), mc_ref[0:1, part])
        target = rew_ref[0:1, part] + 0.98 * (1.0 - term_ref[0:1, part].astype(F32)) * bootstrap
        tgt_ref[0:1, part] = used * target
        taken = jax.nn.sigmoid(tk[0:1, part])
        errors = used * 2.0 * (taken - target) * taken * (1.0 - taken) * gain
        pieces.append(jnp.where(bin_ids == act_ref[0:1, part], errors, 0.0).astype(BF16))
    d_logits_t = jnp.concatenate(pieces, axis=1)
    back_t = jnp.dot(wout_ref[...], d_logits_t, preferred_element_type=F32)
    dh_t[...] = (back_t * slope_t[...]).astype(BF16)
    gout[...] = jnp.dot(d_logits_t, hid[...], preferred_element_type=F32).T

    def grad_of(k):
        cols = pl.ds(pl.multiple_of(k * share, share), share)
        return jnp.dot(dh_t[...], cur[:, cols], preferred_element_type=F32)

    def out_rows(k, j):
        return gout[pl.ds(pl.multiple_of(k * (half * side) + j * half, half), half), :]

    def core_copy(s):
        return pltpu.make_async_remote_copy(
            src_ref=core_src.at[s], dst_ref=core_got.at[s], send_sem=core_ss.at[s], recv_sem=core_rs.at[s],
            device_id={"rep": chip * 2 + 1 - core}, device_id_type=MESH,
        )

    def chip_copy(s, there):
        return pltpu.make_async_remote_copy(
            src_ref=chip_src.at[s], dst_ref=chip_got.at[s], send_sem=chip_ss.at[s], recv_sem=chip_rs.at[s],
            device_id={"rep": there * 2 + core}, device_id_type=MESH,
        )

    order = [flip(chip, d, chips) for d in range(chips - 1, -1, -1)]

    def forward_sum(s):
        core_copy(s).wait()
        if s < chips - 1:
            chip_src[s] = (own[s] + core_got[s].astype(F32)).astype(BF16)
            chip_copy(s, order[s]).start()

    for s in range(chips):
        other, mine_k = order[s] * 2 + 1 - core, order[s] * 2 + core
        core_src[s, 0:head, :] = grad_of(other).astype(BF16)
        for j in range(side):
            core_src[s, head:head + half, j * bins:(j + 1) * bins] = out_rows(other, j).astype(BF16)
        core_copy(s).start()
        own[s, 0:head, :] = grad_of(mine_k)
        for j in range(side):
            own[s, head:head + half, j * bins:(j + 1) * bins] = out_rows(mine_k, j)
        if s > 0:
            forward_sum(s - 1)
    forward_sum(chips - 1)

    total = own[chips - 1] + core_got[chips - 1].astype(F32)
    for s in range(chips - 1):
        chip_copy(s, order[s]).wait()
        total = total + chip_got[s].astype(F32)
    gin_ref[...] = total[0:head, :].T
    for j in range(side):
        gout_ref[j * half:(j + 1) * half, :] = total[head:head + half, j * bins:(j + 1) * bins]
    for d in range(1, n):
        rep_copy(d, me).wait_send()


def shards(
    members, n,
    cur_states, buffer, fetch_rows, fetch_counts, actions, rewards, terminal, mc_return, w_in, w_out
):
    slots, width = cur_states.shape
    rows = buffer.shape[0]
    head, bins = w_out.shape[1:]
    cap = fetch_rows.shape[2]
    chips = n // 2
    share = width // n
    tile = min(256, slots // 2)
    packed = head + head // n // (share // bins)
    vmem, hbm = pl.BlockSpec(memory_space=pltpu.VMEM), pl.BlockSpec(memory_space=pl.ANY)
    dma = pltpu.SemaphoreType.DMA
    targets, grad_first, grad_second = pl.pallas_call(
        functools.partial(kernel, n, members, tile),
        out_shape=(
            jax.ShapeDtypeStruct((1, slots), F32),
            jax.ShapeDtypeStruct((share, head), F32),
            jax.ShapeDtypeStruct((head // n, bins), F32),
        ),
        in_specs=[hbm, hbm, vmem, pl.BlockSpec(memory_space=pltpu.SMEM), vmem, vmem, vmem, vmem, hbm, vmem],
        out_specs=(vmem, vmem, vmem),
        scratch_shapes=[
            pltpu.VMEM((slots, width), BF16),
            pltpu.VMEM((rows, width), BF16),
            pltpu.VMEM((width, head), BF16),
            pltpu.VMEM((bins, head), BF16),
            pltpu.VMEM((slots, head), BF16),
            pltpu.VMEM((head, slots), F32),
            pltpu.VMEM((8, slots), F32),
            pltpu.VMEM((head, slots), BF16),
            pltpu.VMEM((head, bins), F32),
            pltpu.VMEM((8, rows), F32),
            pltpu.VMEM((members - 1, 8, rows), F32),
            pltpu.VMEM((n, 8, cap), F32),
            pltpu.VMEM((n, 8, cap), F32),
            pltpu.VMEM((chips, packed, share), F32),
            pltpu.VMEM((chips, packed, share), BF16),
            pltpu.VMEM((chips, packed, share), BF16),
            pltpu.VMEM((chips - 1, packed, share), BF16),
            pltpu.VMEM((chips - 1, packed, share), BF16),
            dma((2,)), dma((slots // tile,)),
            dma((members - 1,)), dma((members - 1,)),
            dma((n - 1,)), dma((n,)),
            dma((chips,)), dma((chips,)),
            dma((chips - 1,)), dma((chips - 1,)),
        ],
        compiler_params=pltpu.CompilerParams(
            collective_id=0, has_side_effects=True, vmem_limit_bytes=60 * 1024 * 1024
        ),
    )(
        cur_states, buffer, fetch_rows[0], fetch_counts,
        actions.reshape(1, slots), rewards.reshape(1, slots), terminal.reshape(1, slots), mc_return.reshape(1, slots),
        w_in[0], w_out[0],
    )
    return targets.reshape(slots), grad_first[None], grad_second[None]


def solution(mesh):
    placed = (
        P("rep", None),
        P("rep", None),
        P("rep", None, None),
        P(),
        P("rep"),
        P("rep"),
        P("rep"),
        P("rep"),
        P("ens", None, None),
        P("ens", None, None),
    )
    return jax.shard_map(
        functools.partial(shards, mesh.shape["ens"], mesh.shape["rep"]),
        mesh=mesh,
        in_specs=placed,
        out_specs=(P("rep"), P("ens", "rep", None), P("ens", "rep", None)),
        check_vma=False,
    )
```

time: 184 us -> 55.7 us (0.30)
  waiting for transfers between devices: 104 us -> 0 us
  Pallas kernels: 0 us -> 49.8 us
  matrix products: 34.2 us -> 0 us
  between operations: 14.8 us -> 0.64 us
  blocking collectives: 12 us -> 0 us
  local copies, waits for them, and re-layouts: 10.5 us -> 5.01 us
  starting transfers between devices: 5.26 us -> 0 us
  other arithmetic: 2.92 us -> 0 us
    reduce_scatter x2 -> x0, waiting for transfers between devices: 104 us -> none  [the longest x1 68.1 us: shards(): lax.psum_scatter(grad_first, 'rep', scatter_dimension=0, tiled=True)]
    pallas_call x0 -> x1, Pallas kernels: none -> 49.8 us  [shards(): pl.pallas_call(functools.partial(kernel, n, members, tile), out_shape=(ja...]
    dot_general x5 -> x0, matrix products: 34.2 us -> none  [the longest x1 11.2 us: shards(): lax.dot_general(cur_states, d_hidden, (((0,), (0,)), ((), ())), preferred...]
    pmin x1 -> x0, blocking collectives: 12 us -> none  [shards(): ens_floor = lax.pmin(best_next, 'ens')]
    gather x1 -> x0, local copies, waits for them, and re-layouts: 7.73 us -> none  [shards(): jnp.take(buffer, fetch_rows[0].reshape(-1), axis=0)]
    all_to_all x1 -> x0, starting transfers between devices: 5.17 us -> none  [shards(): lax.all_to_all(served, 'rep', split_axis=0, concat_axis=0, tiled=True)]
    unnamed x15 -> x3, local copies, waits for them, and re-layouts: 2.62 us -> 5.01 us
  transfers between devices with their start and end apart: 3 -> 0, of which waited for: 2 -> 0; matrix products, arithmetic and copies ran while one was open for 9% -> 0% of each run, Pallas kernels for 0% -> 0%
where the time goes in v1:
time: 55.7 us; the launch traced here: 55.4 us
  Pallas kernels  49.8 us (89%)
  local copies, waits for them, and re-layouts  5.01 us (9%)
  between operations  0.64 us (1%)
    pallas_call x1, Pallas kernels, shards(): pl.pallas_call(functools.partial(kernel, n, members, tile), out_shape=(ja...  49.8 us
    unnamed x3, local copies, waits for them, and re-layouts  5.01 us

profile of v1, /device:TPU:0, one launch (start us, length us, event | category | flops | bytes accessed | tf_op | source)
XLA Modules:
  0.0 55.4 jit_solution(3527173484914342775)
XLA Ops:
  0.6 49.8 %shard_map.121 = (f32[1,1024]{1,0:T(1,128)}, f32[512,512]{1,0:T(8,128)}, f32[64,256]{1,0:T(8,128)}) custom-call(bf16[1024,4096]{1,0:T(8,128)(2,1)} %cur_hbm.1, bf16[256,4096]{1,0:T(8,128)(2,1)} %buf_hbm.1, s32[8,128]{1,0:T(8,128)} %bitcast.15, s32[8,8]{1,0:T(8,128)} %counts_ref.1, s32[1,1024]{1,0:T(1,128)} %bitcast.16, f32[1,1024]{1,0:T(1,128)} %bitcast.17, ...), custom_call_target="tpu_custom_call" | custom-call | tf_op jit(solution)/shard_map/pallas_call | solution.py:214
  50.4 1.3 %copy.16 = f32[1024]{0:T(1024)} copy(f32[1024]{0:T(1024)} %bitcast.14) | data formatting | bytes 8192
  51.7 2.3 %copy.17 = f32[1,512,512]{2,1,0:T(8,128)} copy(f32[1,512,512]{2,1,0:T(8,128)} %bitcast.11) | data formatting | bytes 2097152
  53.9 1.5 %copy.18 = f32[1,64,256]{2,1,0:T(8,128)} copy(f32[1,64,256]{2,1,0:T(8,128)} %bitcast.13) | data formatting | bytes 131072

commit v2 on v1

--- a/solution.py
+++ b/solution.py
@@ -21,9 +21,9 @@
 
 
 def kernel(
-    n, members, tile,
+    n, members, tile, parts,
     cur_hbm, buf_hbm, fetch_ref, counts_ref, act_ref, rew_ref, term_ref, mc_ref, win_hbm, wout_ref,
-    tgt_ref, gin_ref, gout_ref,
+    tgt_ref, tot_ref,
     cur, buf, win, wout_t, hid, slope_t, tk, dh_t, gout, mine, ens_got, serve, got,
     own, core_src, core_got, chip_src, chip_got,
     in_sem, cur_sem, ens_ss, ens_rs, rep_ss, rep_rs, core_ss, core_rs, chip_ss, chip_rs,
@@ -38,19 +38,29 @@
     chip, core = me // 2, me % 2
     share = width // n
     side = share // bins
-    half = head // n // side
-
-    load_win = pltpu.make_async_copy(win_hbm, win, in_sem.at[0])
-    load_buf = pltpu.make_async_copy(buf_hbm, buf, in_sem.at[1])
-    load_win.start()
-    load_buf.start()
+    upper, lower = head // 2, head // n // (2 * side)
+    steps, relay = steps_of(chips)
+
+    def relayed(d):
+        return relay and d == 3
+
+    depth = width // parts
+
+    def load_win(k):
+        part = slice(k * depth, (k + 1) * depth)
+        return pltpu.make_async_copy(win_hbm.at[part], win.at[part], in_sem.at[2 * k])
+
+    def load_buf(k):
+        part = slice(k * depth, (k + 1) * depth)
+        return pltpu.make_async_copy(buf_hbm.at[:, part], buf.at[:, part], in_sem.at[2 * k + 1])
+
+    for k in range(parts):
+        load_win(k).start()
+        load_buf(k).start()
 
     def load_cur(i):
         part = pl.ds(pl.multiple_of(i * tile, tile), tile)
         return pltpu.make_async_copy(cur_hbm.at[part], cur.at[part], cur_sem.at[i])
-
-    for i in range(tiles):
-        load_cur(i).start()
 
     barrier = pltpu.get_barrier_semaphore()
     for d in range(1, members):
@@ -70,9 +80,16 @@
             wout_t[...], hidden, (((1,), (1,)), ((), ())), preferred_element_type=F32
         )
 
-    load_win.wait()
-    load_buf.wait()
-    pre = jnp.dot(buf[...], win[...], preferred_element_type=F32)
+    pre = None
+    for k in range(parts):
+        load_win(k).wait()
+        load_buf(k).wait()
+        if k == min(1, parts - 1):
+            for i in range(tiles):
+                load_cur(i).start()
+        part = slice(k * depth, (k + 1) * depth)
+        term = jnp.dot(buf[:, part], win[part, :], preferred_element_type=F32)
+        pre = term if pre is None else pre + term
     hidden = (pre * jax.nn.sigmoid(pre)).astype(BF16)
     best = jnp.max(logits_of(hidden), axis=0, keepdims=True)
     mine[...] = jnp.broadcast_to(best, mine.shape)
@@ -146,55 +163,95 @@
     dh_t[...] = (back_t * slope_t[...]).astype(BF16)
     gout[...] = jnp.dot(d_logits_t, hid[...], preferred_element_type=F32).T
 
-    def grad_of(k):
+    def grad_of(k, p):
         cols = pl.ds(pl.multiple_of(k * share, share), share)
-        return jnp.dot(dh_t[...], cur[:, cols], preferred_element_type=F32)
-
-    def out_rows(k, j):
-        return gout[pl.ds(pl.multiple_of(k * (half * side) + j * half, half), half), :]
-
-    def core_copy(s):
+        return jnp.dot(dh_t[p * upper:(p + 1) * upper, :], cur[:, cols], preferred_element_type=F32)
+
+    def out_rows(k, p, j):
+        first = k * (2 * side * lower) + (p * side + j) * lower
+        return gout[pl.ds(pl.multiple_of(first, lower), lower), :]
+
+    def core_copy(i):
         return pltpu.make_async_remote_copy(
-            src_ref=core_src.at[s], dst_ref=core_got.at[s], send_sem=core_ss.at[s], recv_sem=core_rs.at[s],
+            src_ref=core_src.at[i], dst_ref=core_got.at[i], send_sem=core_ss.at[i], recv_sem=core_rs.at[i],
             device_id={"rep": chip * 2 + 1 - core}, device_id_type=MESH,
         )
 
-    def chip_copy(s, there):
+    def chip_copy(i):
+        d, p = steps[i]
+        there = flip(chip, p + 1 if relayed(d) else d, chips)
         return pltpu.make_async_remote_copy(
-            src_ref=chip_src.at[s], dst_ref=chip_got.at[s], send_sem=chip_ss.at[s], recv_sem=chip_rs.at[s],
+            src_ref=chip_src.at[i], dst_ref=chip_got.at[i], send_sem=chip_ss.at[i], recv_sem=chip_rs.at[i],
             device_id={"rep": there * 2 + core}, device_id_type=MESH,
         )
 
-    order = [flip(chip, d, chips) for d in range(chips - 1, -1, -1)]
-
-    def forward_sum(s):
-        core_copy(s).wait()
-        if s < chips - 1:
-            chip_src[s] = (own[s] + core_got[s].astype(F32)).astype(BF16)
-            chip_copy(s, order[s]).start()
-
-    for s in range(chips):
-        other, mine_k = order[s] * 2 + 1 - core, order[s] * 2 + core
-        core_src[s, 0:head, :] = grad_of(other).astype(BF16)
-        for j in range(side):
-            core_src[s, head:head + half, j * bins:(j + 1) * bins] = out_rows(other, j).astype(BF16)
-        core_copy(s).start()
-        own[s, 0:head, :] = grad_of(mine_k)
-        for j in range(side):
-            own[s, head:head + half, j * bins:(j + 1) * bins] = out_rows(mine_k, j)
-        if s > 0:
-            forward_sum(s - 1)
-    forward_sum(chips - 1)
-
-    total = own[chips - 1] + core_got[chips - 1].astype(F32)
-    for s in range(chips - 1):
-        chip_copy(s, order[s]).wait()
-        total = total + chip_got[s].astype(F32)
-    gin_ref[...] = total[0:head, :].T
-    for j in range(side):
-        gout_ref[j * half:(j + 1) * half, :] = total[head:head + half, j * bins:(j + 1) * bins]
+    def compute(i):
+        d, p = steps[i]
+        there = flip(chip, d, chips)
+        for k, dst in ((there * 2 + 1 - core, core_src), (there * 2 + core, own)):
+            dst[i, 0:upper, :] = grad_of(k, p).astype(dst.dtype)
+            for j in range(side):
+                dst[i, upper:upper + lower, j * bins:(j + 1) * bins] = out_rows(k, p, j).astype(dst.dtype)
+            if dst is core_src:
+                core_copy(i).start()
+
+    def pass_on(i):
+        d, p = steps[i]
+        core_copy(i).wait()
+        value = own[i] + core_got[i].astype(F32)
+        if d == 0:
+            own[i] = value
+            return
+        if relay and (d, p) in ((1, 1), (2, 0)):
+            came = steps.index((3, p))
+            chip_copy(came).wait_recv()
+            value = value + chip_got[came].astype(F32)
+        chip_src[i] = value.astype(BF16)
+        chip_copy(i).start()
+
+    last = len(steps) - 1
+    late = [i for i in range(last + 1) if relay and steps[i] in ((1, 1), (2, 0))]
+    for i in range(last + 1):
+        compute(i)
+        if i > 0 and i - 1 not in late:
+            pass_on(i - 1)
+    pass_on(last)
+    for i in late:
+        pass_on(i)
+
+    for i in range(last - 1):
+        d, p = steps[i]
+        if relayed(d):
+            chip_copy(i).wait_send()
+            continue
+        chip_copy(i).wait()
+        if i not in late:
+            own[last - 1 + p] = own[last - 1 + p] + chip_got[i].astype(F32)
+    for p in range(2):
+        total = own[last - 1 + p]
+        for i in late:
+            if steps[i][1] == p:
+                total = total + chip_got[i].astype(F32)
+        tot_ref[p] = total
     for d in range(1, n):
         rep_copy(d, me).wait_send()
+
+
+def steps_of(chips):
+    if chips == 4:
+        return [(3, 0), (3, 1), (1, 0), (2, 1), (1, 1), (2, 0), (0, 0), (0, 1)], True
+    return [(d, p) for d in range(chips - 1, -1, -1) for p in range(2)], False
+
+
+def unpack(side, tgt_in, tot, tgt_ref, gin_ref, gout_ref):
+    upper, lower = gin_ref.shape[1] // 2, gout_ref.shape[0] // (2 * side)
+    bins = gout_ref.shape[1]
+    tgt_ref[...] = tgt_in[...]
+    for p in range(2):
+        gin_ref[:, p * upper:(p + 1) * upper] = tot[p, 0:upper, :].T
+        for j in range(side):
+            first = (p * side + j) * lower
+            gout_ref[first:first + lower, :] = tot[p, upper:upper + lower, j * bins:(j + 1) * bins]
 
 
 def shards(
@@ -208,18 +265,20 @@
     chips = n // 2
     share = width // n
     tile = min(256, slots // 2)
-    packed = head + head // n // (share // bins)
+    side = share // bins
+    packed = head // 2 + head // n // (2 * side)
+    count = len(steps_of(chips)[0])
+    parts = 4
     vmem, hbm = pl.BlockSpec(memory_space=pltpu.VMEM), pl.BlockSpec(memory_space=pl.ANY)
     dma = pltpu.SemaphoreType.DMA
-    targets, grad_first, grad_second = pl.pallas_call(
-        functools.partial(kernel, n, members, tile),
+    targets, totals = pl.pallas_call(
+        functools.partial(kernel, n, members, tile, parts),
         out_shape=(
             jax.ShapeDtypeStruct((1, slots), F32),
-            jax.ShapeDtypeStruct((share, head), F32),
-            jax.ShapeDtypeStruct((head // n, bins), F32),
+            jax.ShapeDtypeStruct((2, packed, share), F32),
         ),
         in_specs=[hbm, hbm, vmem, pl.BlockSpec(memory_space=pltpu.SMEM), vmem, vmem, vmem, vmem, hbm, vmem],
-        out_specs=(vmem, vmem, vmem),
+        out_specs=(vmem, vmem),
         scratch_shapes=[
             pltpu.VMEM((slots, width), BF16),
             pltpu.VMEM((rows, width), BF16),
@@ -234,16 +293,16 @@
             pltpu.VMEM((members - 1, 8, rows), F32),
             pltpu.VMEM((n, 8, cap), F32),
             pltpu.VMEM((n, 8, cap), F32),
-            pltpu.VMEM((chips, packed, share), F32),
-            pltpu.VMEM((chips, packed, share), BF16),
-            pltpu.VMEM((chips, packed, share), BF16),
-            pltpu.VMEM((chips - 1, packed, share), BF16),
-            pltpu.VMEM((chips - 1, packed, share), BF16),
-            dma((2,)), dma((slots // tile,)),
+            pltpu.VMEM((count, packed, share), F32),
+            pltpu.VMEM((count, packed, share), BF16),
+            pltpu.VMEM((count, packed, share), BF16),
+            pltpu.VMEM((count - 2, packed, share), BF16),
+            pltpu.VMEM((count - 2, packed, share), BF16),
+            dma((2 * parts,)), dma((slots // tile,)),
             dma((members - 1,)), dma((members - 1,)),
             dma((n - 1,)), dma((n,)),
-            dma((chips,)), dma((chips,)),
-            dma((chips - 1,)), dma((chips - 1,)),
+            dma((count,)), dma((count,)),
+            dma((count - 2,)), dma((count - 2,)),
         ],
         compiler_params=pltpu.CompilerParams(
             collective_id=0, has_side_effects=True, vmem_limit_bytes=60 * 1024 * 1024
@@ -253,6 +312,17 @@
         actions.reshape(1, slots), rewards.reshape(1, slots), terminal.reshape(1, slots), mc_return.reshape(1, slots),
         w_in[0], w_out[0],
     )
+    targets, grad_first, grad_second = pl.pallas_call(
+        functools.partial(unpack, side),
+        out_shape=(
+            jax.ShapeDtypeStruct((1, slots), F32),
+            jax.ShapeDtypeStruct((share, head), F32),
+            jax.ShapeDtypeStruct((head // n, bins), F32),
+        ),
+        in_specs=[vmem, vmem],
+        out_specs=(vmem, vmem, vmem),
+        compiler_params=pltpu.CompilerParams(vmem_limit_bytes=60 * 1024 * 1024),
+    )(targets, totals)
     return targets.reshape(slots), grad_first[None], grad_second[None]
 
 

time: 55.7 us -> 43.6 us (0.78)
  Pallas kernels: 49.8 us -> 42.8 us
  local copies, waits for them, and re-layouts: 5.01 us -> 0 us
    pallas_call x1 -> x2, Pallas kernels: 49.8 us -> 42.8 us  [the longest x1 40.3 us: shards(): pl.pallas_call(functools.partial(kernel, n, members, tile, parts), out_sh...]
    unnamed x3 -> x0, local copies, waits for them, and re-layouts: 5.01 us -> none
where the time goes in v2:
time: 43.6 us; the launch traced here: 43.5 us
  Pallas kernels  42.8 us (98%)
  between operations  0.64 us (1%)
    pallas_call x1, Pallas kernels, shards(): pl.pallas_call(functools.partial(kernel, n, members, tile, parts), out_sh...  40.3 us
    pallas_call x1, Pallas kernels, shards(): pl.pallas_call(functools.partial(unpack, side), out_shape=(jax.ShapeDtype...  2.56 us

profile of v2, /device:TPU:0, one launch (start us, length us, event | category | flops | bytes accessed | tf_op | source)
XLA Modules:
  0.0 43.5 jit_solution(7535371238440384309)
XLA Ops:
  0.6 40.3 %shard_map.121 = (f32[1,1024]{1,0:T(1,128)}, f32[2,272,512]{2,1,0:T(8,128)}) custom-call(bf16[1024,4096]{1,0:T(8,128)(2,1)} %cur_hbm.1, bf16[256,4096]{1,0:T(8,128)(2,1)} %buf_hbm.1, s32[8,128]{1,0:T(8,128)} %bitcast.12, s32[8,8]{1,0:T(8,128)} %counts_ref.1, s32[1,1024]{1,0:T(1,128)} %bitcast.13, f32[1,1024]{1,0:T(1,128)} %bitcast.14, s32[1,1024]{1,0:T(1,128)} %bitcast.15, ...), custom_call_target="tpu_custom_call" | custom-call | tf_op jit(solution)/shard_map/pallas_call | solution.py:274
  40.9 2.6 %shard_map.122 = (f32[1,1024]{1,0:T(1,128)}, f32[512,512]{1,0:T(8,128)}, f32[64,256]{1,0:T(8,128)}) custom-call(f32[1,1024]{1,0:T(1,128)} %get-tuple-element.8.tgt_in, f32[2,272,512]{2,1,0:T(8,128)} %get-tuple-element.9.tot), custom_call_target="tpu_custom_call" | custom-call | tf_op jit(solution)/shard_map/pallas_call | solution.py:315

commit v3 on v2

--- a/solution.py
+++ b/solution.py
@@ -21,24 +21,23 @@
 
 
 def kernel(
-    n, members, tile, parts,
+    n, members, first, parts,
     cur_hbm, buf_hbm, fetch_ref, counts_ref, act_ref, rew_ref, term_ref, mc_ref, win_hbm, wout_ref,
     tgt_ref, tot_ref,
-    cur, buf, win, wout_t, hid, slope_t, tk, dh_t, gout, mine, ens_got, serve, got,
+    states, pre, win, wout_t, hid, slope_t, tk, dh_t, gout, mine, ens_got, serve, got,
     own, core_src, core_got, chip_src, chip_got,
     in_sem, cur_sem, ens_ss, ens_rs, rep_ss, rep_rs, core_ss, core_rs, chip_ss, chip_rs,
 ):
     me, member = lax.axis_index("rep"), lax.axis_index("ens")
-    slots, width = cur.shape
     head, bins = wout_ref.shape
     cap = fetch_ref.shape[1]
-    rows = buf.shape[0]
-    tiles = slots // tile
+    slots, width = cur_hbm.shape
+    rows = buf_hbm.shape[0]
     chips = n // 2
     chip, core = me // 2, me % 2
     share = width // n
     side = share // bins
-    upper, lower = head // 2, head // n // (2 * side)
+    upper, lower = head // 2, head // n // side
     steps, relay = steps_of(chips)
 
     def relayed(d):
@@ -52,15 +51,21 @@
 
     def load_buf(k):
         part = slice(k * depth, (k + 1) * depth)
-        return pltpu.make_async_copy(buf_hbm.at[:, part], buf.at[:, part], in_sem.at[2 * k + 1])
-
+        return pltpu.make_async_copy(buf_hbm.at[:, part], states.at[0:rows, part], in_sem.at[2 * k + 1])
+
+    def load_early(k):
+        part = slice(k * depth, (k + 1) * depth)
+        return pltpu.make_async_copy(
+            cur_hbm.at[0:first, part], states.at[rows:rows + first, part], cur_sem.at[k]
+        )
+
+    load_late = pltpu.make_async_copy(
+        cur_hbm.at[first:slots], states.at[rows + first:rows + slots], cur_sem.at[parts]
+    )
     for k in range(parts):
         load_win(k).start()
         load_buf(k).start()
-
-    def load_cur(i):
-        part = pl.ds(pl.multiple_of(i * tile, tile), tile)
-        return pltpu.make_async_copy(cur_hbm.at[part], cur.at[part], cur_sem.at[i])
+        load_early(k).start()
 
     barrier = pltpu.get_barrier_semaphore()
     for d in range(1, members):
@@ -75,23 +80,44 @@
             counted = counted + counts_ref[a, b]
     gain = 65536.0 / jnp.full((1, cap), counted, jnp.int32).astype(F32)
 
-    def logits_of(hidden):
+    def activate(begin, end):
+        for top in range(begin, end, 128):
+            down = slice(top, top + 128)
+            for left in range(0, head, 128):
+                across = slice(left, left + 128)
+                x = pre[down, across]
+                sig = jax.nn.sigmoid(x)
+                hid[down, across] = (x * sig).astype(BF16)
+                if top >= rows:
+                    slope_t[across, top - rows:top - rows + 128] = (sig * (1.0 + x * (1.0 - sig))).T
+
+    def logits_of(begin, end):
         return lax.dot_general(
-            wout_t[...], hidden, (((1,), (1,)), ((), ())), preferred_element_type=F32
-        )
-
-    pre = None
+            wout_t[...], hid[begin:end, :], (((1,), (1,)), ((), ())), preferred_element_type=F32
+        )
+
+    def take(begin, end):
+        logits = logits_of(rows + begin, rows + end)
+        ids = lax.broadcasted_iota(jnp.int32, (bins, 128), 0)
+        for left in range(0, end - begin, 128):
+            part = slice(begin + left, begin + left + 128)
+            picked = jnp.where(ids == act_ref[0:1, part], logits[:, left:left + 128], 0.0)
+            tk[0:1, part] = jnp.sum(picked, axis=0, keepdims=True)
+
     for k in range(parts):
         load_win(k).wait()
         load_buf(k).wait()
+        load_early(k).wait()
         if k == min(1, parts - 1):
-            for i in range(tiles):
-                load_cur(i).start()
+            load_late.start()
         part = slice(k * depth, (k + 1) * depth)
-        term = jnp.dot(buf[:, part], win[part, :], preferred_element_type=F32)
-        pre = term if pre is None else pre + term
-    hidden = (pre * jax.nn.sigmoid(pre)).astype(BF16)
-    best = jnp.max(logits_of(hidden), axis=0, keepdims=True)
+        term = jnp.dot(states[0:rows + first, part], win[part, :], preferred_element_type=F32)
+        if k == 0:
+            pre[0:rows + first, :] = term
+        else:
+            pre[0:rows + first, :] += term
+    activate(0, rows)
+    best = jnp.max(logits_of(0, rows), axis=0, keepdims=True)
     mine[...] = jnp.broadcast_to(best, mine.shape)
     pl.semaphore_wait(barrier, members - 1 + n - 1)
 
@@ -104,20 +130,8 @@
     for d in range(1, members):
         ens_copy(d).start()
 
-    def forward(i, carry):
-        load_cur(i).wait()
-        part = pl.ds(pl.multiple_of(i * tile, tile), tile)
-        pre = jnp.dot(cur[part, :], win[...], preferred_element_type=F32)
-        sig = jax.nn.sigmoid(pre)
-        hidden = (pre * sig).astype(BF16)
-        hid[part, :] = hidden
-        slope_t[:, part] = (sig * (1.0 + pre * (1.0 - sig))).T
-        logits = logits_of(hidden)
-        chosen = lax.broadcasted_iota(jnp.int32, (bins, tile), 0) == act_ref[0:1, part]
-        tk[0:1, part] = jnp.sum(jnp.where(chosen, logits, 0.0), axis=0, keepdims=True)
-        return carry
-
-    lax.fori_loop(0, tiles // 2, forward, 0)
+    activate(rows, rows + first)
+    take(0, first)
 
     floor = mine[0:1, :]
     for d in range(1, members):
@@ -142,7 +156,12 @@
         rep_copy(d, me).start()
     got[me] = serve[me]
 
-    lax.fori_loop(tiles // 2, tiles, forward, 0)
+    load_late.wait()
+    pre[rows + first:rows + slots, :] = jnp.dot(
+        states[rows + first:rows + slots, :], win[...], preferred_element_type=F32
+    )
+    activate(rows + first, rows + slots)
+    take(first, slots)
 
     for d in range(1, n):
         rep_copy(d, (me + n - d) % n).wait_recv()
@@ -159,21 +178,25 @@
         errors = used * 2.0 * (taken - target) * taken * (1.0 - taken) * gain
         pieces.append(jnp.where(bin_ids == act_ref[0:1, part], errors, 0.0).astype(BF16))
     d_logits_t = jnp.concatenate(pieces, axis=1)
-    back_t = jnp.dot(wout_ref[...], d_logits_t, preferred_element_type=F32)
-    dh_t[...] = (back_t * slope_t[...]).astype(BF16)
-    gout[...] = jnp.dot(d_logits_t, hid[...], preferred_element_type=F32).T
+
+    def back(p):
+        part = slice(p * upper, (p + 1) * upper)
+        back_t = jnp.dot(wout_ref[part, :], d_logits_t, preferred_element_type=F32)
+        dh_t[part, :] = (back_t * slope_t[part, :]).astype(BF16)
 
     def grad_of(k, p):
         cols = pl.ds(pl.multiple_of(k * share, share), share)
-        return jnp.dot(dh_t[p * upper:(p + 1) * upper, :], cur[:, cols], preferred_element_type=F32)
-
-    def out_rows(k, p, j):
-        first = k * (2 * side * lower) + (p * side + j) * lower
-        return gout[pl.ds(pl.multiple_of(first, lower), lower), :]
+        return jnp.dot(dh_t[p * upper:(p + 1) * upper, :], states[rows:rows + slots, cols], preferred_element_type=F32)
+
+    def out_rows(k, j):
+        return gout[pl.ds(pl.multiple_of((k * side + j) * lower, lower), lower), :]
+
+    def size(i):
+        return upper + lower * steps[i][1]
 
     def core_copy(i):
         return pltpu.make_async_remote_copy(
-            src_ref=core_src.at[i], dst_ref=core_got.at[i], send_sem=core_ss.at[i], recv_sem=core_rs.at[i],
+            src_ref=core_src.at[i, 0:size(i)], dst_ref=core_got.at[i, 0:size(i)], send_sem=core_ss.at[i], recv_sem=core_rs.at[i],
             device_id={"rep": chip * 2 + 1 - core}, device_id_type=MESH,
         )
 
@@ -181,7 +204,7 @@
         d, p = steps[i]
         there = flip(chip, p + 1 if relayed(d) else d, chips)
         return pltpu.make_async_remote_copy(
-            src_ref=chip_src.at[i], dst_ref=chip_got.at[i], send_sem=chip_ss.at[i], recv_sem=chip_rs.at[i],
+            src_ref=chip_src.at[i, 0:size(i)], dst_ref=chip_got.at[i, 0:size(i)], send_sem=chip_ss.at[i], recv_sem=chip_rs.at[i],
             device_id={"rep": there * 2 + core}, device_id_type=MESH,
         )
 
@@ -190,28 +213,33 @@
         there = flip(chip, d, chips)
         for k, dst in ((there * 2 + 1 - core, core_src), (there * 2 + core, own)):
             dst[i, 0:upper, :] = grad_of(k, p).astype(dst.dtype)
-            for j in range(side):
-                dst[i, upper:upper + lower, j * bins:(j + 1) * bins] = out_rows(k, p, j).astype(dst.dtype)
+            for j in range(side * p):
+                dst[i, upper:upper + lower, j * bins:(j + 1) * bins] = out_rows(k, j).astype(dst.dtype)
             if dst is core_src:
                 core_copy(i).start()
 
     def pass_on(i):
         d, p = steps[i]
         core_copy(i).wait()
-        value = own[i] + core_got[i].astype(F32)
+        size_i = size(i)
+        value = own[i, 0:size_i] + core_got[i, 0:size_i].astype(F32)
         if d == 0:
-            own[i] = value
+            own[i, 0:size_i] = value
             return
         if relay and (d, p) in ((1, 1), (2, 0)):
             came = steps.index((3, p))
             chip_copy(came).wait_recv()
-            value = value + chip_got[came].astype(F32)
-        chip_src[i] = value.astype(BF16)
+            value = value + chip_got[came, 0:size_i].astype(F32)
+        chip_src[i, 0:size_i] = value.astype(BF16)
         chip_copy(i).start()
 
     last = len(steps) - 1
     late = [i for i in range(last + 1) if relay and steps[i] in ((1, 1), (2, 0))]
+    back(0)
     for i in range(last + 1):
+        if i == 1:
+            back(1)
+            gout[...] = jnp.dot(d_logits_t, hid[rows:rows + slots, :], preferred_element_type=F32).T
         compute(i)
         if i > 0 and i - 1 not in late:
             pass_on(i - 1)
@@ -226,13 +254,15 @@
             continue
         chip_copy(i).wait()
         if i not in late:
-            own[last - 1 + p] = own[last - 1 + p] + chip_got[i].astype(F32)
+            size_i = size(i)
+            own[last - 1 + p, 0:size_i] = own[last - 1 + p, 0:size_i] + chip_got[i, 0:size_i].astype(F32)
     for p in range(2):
-        total = own[last - 1 + p]
+        size_p = size(last - 1 + p)
+        total = own[last - 1 + p, 0:size_p]
         for i in late:
             if steps[i][1] == p:
-                total = total + chip_got[i].astype(F32)
-        tot_ref[p] = total
+                total = total + chip_got[i, 0:size_p].astype(F32)
+        tot_ref[p, 0:size_p] = total
     for d in range(1, n):
         rep_copy(d, me).wait_send()
 
@@ -244,14 +274,13 @@
 
 
 def unpack(side, tgt_in, tot, tgt_ref, gin_ref, gout_ref):
-    upper, lower = gin_ref.shape[1] // 2, gout_ref.shape[0] // (2 * side)
+    upper, lower = gin_ref.shape[1] // 2, gout_ref.shape[0] // side
     bins = gout_ref.shape[1]
     tgt_ref[...] = tgt_in[...]
     for p in range(2):
         gin_ref[:, p * upper:(p + 1) * upper] = tot[p, 0:upper, :].T
-        for j in range(side):
-            first = (p * side + j) * lower
-            gout_ref[first:first + lower, :] = tot[p, upper:upper + lower, j * bins:(j + 1) * bins]
+    for j in range(side):
+        gout_ref[j * lower:(j + 1) * lower, :] = tot[1, upper:upper + lower, j * bins:(j + 1) * bins]
 
 
 def shards(
@@ -264,15 +293,15 @@
     cap = fetch_rows.shape[2]
     chips = n // 2
     share = width // n
-    tile = min(256, slots // 2)
+    first = slots * 3 // 8 // 128 * 128
     side = share // bins
-    packed = head // 2 + head // n // (2 * side)
+    packed = head // 2 + head // n // side
     count = len(steps_of(chips)[0])
     parts = 4
     vmem, hbm = pl.BlockSpec(memory_space=pltpu.VMEM), pl.BlockSpec(memory_space=pl.ANY)
     dma = pltpu.SemaphoreType.DMA
     targets, totals = pl.pallas_call(
-        functools.partial(kernel, n, members, tile, parts),
+        functools.partial(kernel, n, members, first, parts),
         out_shape=(
             jax.ShapeDtypeStruct((1, slots), F32),
             jax.ShapeDtypeStruct((2, packed, share), F32),
@@ -280,11 +309,11 @@
         in_specs=[hbm, hbm, vmem, pl.BlockSpec(memory_space=pltpu.SMEM), vmem, vmem, vmem, vmem, hbm, vmem],
         out_specs=(vmem, vmem),
         scratch_shapes=[
-            pltpu.VMEM((slots, width), BF16),
-            pltpu.VMEM((rows, width), BF16),
+            pltpu.VMEM((rows + slots, width), BF16),
+            pltpu.VMEM((rows + slots, head), F32),
             pltpu.VMEM((width, head), BF16),
             pltpu.VMEM((bins, head), BF16),
-            pltpu.VMEM((slots, head), BF16),
+            pltpu.VMEM((rows + slots, head), BF16),
             pltpu.VMEM((head, slots), F32),
             pltpu.VMEM((8, slots), F32),
             pltpu.VMEM((head, slots), BF16),
@@ -298,7 +327,7 @@
             pltpu.VMEM((count, packed, share), BF16),
             pltpu.VMEM((count - 2, packed, share), BF16),
             pltpu.VMEM((count - 2, packed, share), BF16),
-            dma((2 * parts,)), dma((slots // tile,)),
+            dma((2 * parts,)), dma((parts + 1,)),
             dma((members - 1,)), dma((members - 1,)),
             dma((n - 1,)), dma((n,)),
             dma((count,)), dma((count,)),

time: 43.6 us -> 45.5 us (1.044)
  Pallas kernels: 42.8 us -> 44.6 us
    pallas_call x1, Pallas kernels: 40.3 us -> 42.1 us  [shards(): pl.pallas_call(functools.partial(kernel, n, members, first, parts), out_s...]
where the time goes in v3:
time: 45.5 us; the launch traced here: 45.3 us
  Pallas kernels  44.6 us (98%)
  between operations  0.64 us (1%)
    pallas_call x1, Pallas kernels, shards(): pl.pallas_call(functools.partial(kernel, n, members, first, parts), out_s...  42.1 us
    pallas_call x1, Pallas kernels, shards(): pl.pallas_call(functools.partial(unpack, side), out_shape=(jax.ShapeDtype...  2.59 us

profile of v3, /device:TPU:0, one launch (start us, length us, event | category | flops | bytes accessed | tf_op | source)
XLA Modules:
  0.0 45.3 jit_solution(2107107880499270080)
XLA Ops:
  0.6 42.1 %shard_map.121 = (f32[1,1024]{1,0:T(1,128)}, f32[2,288,512]{2,1,0:T(8,128)}) custom-call(bf16[1024,4096]{1,0:T(8,128)(2,1)} %cur_hbm.1, bf16[256,4096]{1,0:T(8,128)(2,1)} %buf_hbm.1, s32[8,128]{1,0:T(8,128)} %bitcast.12, s32[8,8]{1,0:T(8,128)} %counts_ref.1, s32[1,1024]{1,0:T(1,128)} %bitcast.13, f32[1,1024]{1,0:T(1,128)} %bitcast.14, s32[1,1024]{1,0:T(1,128)} %bitcast.15, ...), custom_call_target="tpu_custom_call" | custom-call | tf_op jit(solution)/shard_map/pallas_call | solution.py:303
  42.7 2.6 %shard_map.122 = (f32[1,1024]{1,0:T(1,128)}, f32[512,512]{1,0:T(8,128)}, f32[64,256]{1,0:T(8,128)}) custom-call(f32[1,1024]{1,0:T(1,128)} %get-tuple-element.8.tgt_in, f32[2,288,512]{2,1,0:T(8,128)} %get-tuple-element.9.tot), custom_call_target="tpu_custom_call" | custom-call | tf_op jit(solution)/shard_map/pallas_call | solution.py:344

commit v4 on v2

--- a/solution.py
+++ b/solution.py
@@ -38,7 +38,7 @@
     chip, core = me // 2, me % 2
     share = width // n
     side = share // bins
-    upper, lower = head // 2, head // n // (2 * side)
+    upper, lower = head // 2, head // n // side
     steps, relay = steps_of(chips)
 
     def relayed(d):
@@ -159,21 +159,25 @@
         errors = used * 2.0 * (taken - target) * taken * (1.0 - taken) * gain
         pieces.append(jnp.where(bin_ids == act_ref[0:1, part], errors, 0.0).astype(BF16))
     d_logits_t = jnp.concatenate(pieces, axis=1)
-    back_t = jnp.dot(wout_ref[...], d_logits_t, preferred_element_type=F32)
-    dh_t[...] = (back_t * slope_t[...]).astype(BF16)
-    gout[...] = jnp.dot(d_logits_t, hid[...], preferred_element_type=F32).T
+
+    def back(p):
+        part = slice(p * upper, (p + 1) * upper)
+        back_t = jnp.dot(wout_ref[part, :], d_logits_t, preferred_element_type=F32)
+        dh_t[part, :] = (back_t * slope_t[part, :]).astype(BF16)
 
     def grad_of(k, p):
         cols = pl.ds(pl.multiple_of(k * share, share), share)
         return jnp.dot(dh_t[p * upper:(p + 1) * upper, :], cur[:, cols], preferred_element_type=F32)
 
-    def out_rows(k, p, j):
-        first = k * (2 * side * lower) + (p * side + j) * lower
-        return gout[pl.ds(pl.multiple_of(first, lower), lower), :]
+    def out_rows(k, j):
+        return gout[pl.ds(pl.multiple_of((k * side + j) * lower, lower), lower), :]
+
+    def size(i):
+        return upper + lower * steps[i][1]
 
     def core_copy(i):
         return pltpu.make_async_remote_copy(
-            src_ref=core_src.at[i], dst_ref=core_got.at[i], send_sem=core_ss.at[i], recv_sem=core_rs.at[i],
+            src_ref=core_src.at[i, 0:size(i)], dst_ref=core_got.at[i, 0:size(i)], send_sem=core_ss.at[i], recv_sem=core_rs.at[i],
             device_id={"rep": chip * 2 + 1 - core}, device_id_type=MESH,
         )
 
@@ -181,7 +185,7 @@
         d, p = steps[i]
         there = flip(chip, p + 1 if relayed(d) else d, chips)
         return pltpu.make_async_remote_copy(
-            src_ref=chip_src.at[i], dst_ref=chip_got.at[i], send_sem=chip_ss.at[i], recv_sem=chip_rs.at[i],
+            src_ref=chip_src.at[i, 0:size(i)], dst_ref=chip_got.at[i, 0:size(i)], send_sem=chip_ss.at[i], recv_sem=chip_rs.at[i],
             device_id={"rep": there * 2 + core}, device_id_type=MESH,
         )
 
@@ -190,31 +194,37 @@
         there = flip(chip, d, chips)
         for k, dst in ((there * 2 + 1 - core, core_src), (there * 2 + core, own)):
             dst[i, 0:upper, :] = grad_of(k, p).astype(dst.dtype)
-            for j in range(side):
-                dst[i, upper:upper + lower, j * bins:(j + 1) * bins] = out_rows(k, p, j).astype(dst.dtype)
+            for j in range(side * p):
+                dst[i, upper:upper + lower, j * bins:(j + 1) * bins] = out_rows(k, j).astype(dst.dtype)
             if dst is core_src:
                 core_copy(i).start()
+                if i > 1 and i - 1 not in late:
+                    pass_on(i - 1)
 
     def pass_on(i):
         d, p = steps[i]
         core_copy(i).wait()
-        value = own[i] + core_got[i].astype(F32)
+        size_i = size(i)
+        value = own[i, 0:size_i] + core_got[i, 0:size_i].astype(F32)
         if d == 0:
-            own[i] = value
+            own[i, 0:size_i] = value
             return
         if relay and (d, p) in ((1, 1), (2, 0)):
             came = steps.index((3, p))
             chip_copy(came).wait_recv()
-            value = value + chip_got[came].astype(F32)
-        chip_src[i] = value.astype(BF16)
+            value = value + chip_got[came, 0:size_i].astype(F32)
+        chip_src[i, 0:size_i] = value.astype(BF16)
         chip_copy(i).start()
 
     last = len(steps) - 1
     late = [i for i in range(last + 1) if relay and steps[i] in ((1, 1), (2, 0))]
+    back(0)
     for i in range(last + 1):
+        if i == 1:
+            back(1)
+            gout[...] = jnp.dot(d_logits_t, hid[...], preferred_element_type=F32).T
+            pass_on(0)
         compute(i)
-        if i > 0 and i - 1 not in late:
-            pass_on(i - 1)
     pass_on(last)
     for i in late:
         pass_on(i)
@@ -226,13 +236,15 @@
             continue
         chip_copy(i).wait()
         if i not in late:
-            own[last - 1 + p] = own[last - 1 + p] + chip_got[i].astype(F32)
+            size_i = size(i)
+            own[last - 1 + p, 0:size_i] = own[last - 1 + p, 0:size_i] + chip_got[i, 0:size_i].astype(F32)
     for p in range(2):
-        total = own[last - 1 + p]
+        size_p = size(last - 1 + p)
+        total = own[last - 1 + p, 0:size_p]
         for i in late:
             if steps[i][1] == p:
-                total = total + chip_got[i].astype(F32)
-        tot_ref[p] = total
+                total = total + chip_got[i, 0:size_p].astype(F32)
+        tot_ref[p, 0:size_p] = total
     for d in range(1, n):
         rep_copy(d, me).wait_send()
 
@@ -244,14 +256,13 @@
 
 
 def unpack(side, tgt_in, tot, tgt_ref, gin_ref, gout_ref):
-    upper, lower = gin_ref.shape[1] // 2, gout_ref.shape[0] // (2 * side)
+    upper, lower = gin_ref.shape[1] // 2, gout_ref.shape[0] // side
     bins = gout_ref.shape[1]
     tgt_ref[...] = tgt_in[...]
     for p in range(2):
         gin_ref[:, p * upper:(p + 1) * upper] = tot[p, 0:upper, :].T
-        for j in range(side):
-            first = (p * side + j) * lower
-            gout_ref[first:first + lower, :] = tot[p, upper:upper + lower, j * bins:(j + 1) * bins]
+    for j in range(side):
+        gout_ref[j * lower:(j + 1) * lower, :] = tot[1, upper:upper + lower, j * bins:(j + 1) * bins]
 
 
 def shards(
@@ -266,7 +277,7 @@
     share = width // n
     tile = min(256, slots // 2)
     side = share // bins
-    packed = head // 2 + head // n // (2 * side)
+    packed = head // 2 + head // n // side
     count = len(steps_of(chips)[0])
     parts = 4
     vmem, hbm = pl.BlockSpec(memory_space=pltpu.VMEM), pl.BlockSpec(memory_space=pl.ANY)

time: 43.6 us -> 44.4 us (1.018)
  Pallas kernels: 42.8 us -> 43.6 us
    pallas_call x1, Pallas kernels: 40.3 us -> 41 us  [shards(): pl.pallas_call(functools.partial(kernel, n, members, tile, parts), out_sh...]
where the time goes in v4:
time: 44.4 us; the launch traced here: 44.2 us
  Pallas kernels  43.6 us (98%)
  between operations  0.64 us (1%)
    pallas_call x1, Pallas kernels, shards(): pl.pallas_call(functools.partial(kernel, n, members, tile, parts), out_sh...  41 us
    pallas_call x1, Pallas kernels, shards(): pl.pallas_call(functools.partial(unpack, side), out_shape=(jax.ShapeDtype...  2.59 us

profile of v4, /device:TPU:0, one launch (start us, length us, event | category | flops | bytes accessed | tf_op | source)
XLA Modules:
  0.0 44.2 jit_solution(14387672016649079471)
XLA Ops:
  0.6 41.0 %shard_map.121 = (f32[1,1024]{1,0:T(1,128)}, f32[2,288,512]{2,1,0:T(8,128)}) custom-call(bf16[1024,4096]{1,0:T(8,128)(2,1)} %cur_hbm.1, bf16[256,4096]{1,0:T(8,128)(2,1)} %buf_hbm.1, s32[8,128]{1,0:T(8,128)} %bitcast.12, s32[8,8]{1,0:T(8,128)} %counts_ref.1, s32[1,1024]{1,0:T(1,128)} %bitcast.13, f32[1,1024]{1,0:T(1,128)} %bitcast.14, s32[1,1024]{1,0:T(1,128)} %bitcast.15, ...), custom_call_target="tpu_custom_call" | custom-call | tf_op jit(solution)/shard_map/pallas_call | solution.py:285
  41.6 2.6 %shard_map.122 = (f32[1,1024]{1,0:T(1,128)}, f32[512,512]{1,0:T(8,128)}, f32[64,256]{1,0:T(8,128)}) custom-call(f32[1,1024]{1,0:T(1,128)} %get-tuple-element.8.tgt_in, f32[2,288,512]{2,1,0:T(8,128)} %get-tuple-element.9.tot), custom_call_target="tpu_custom_call" | custom-call | tf_op jit(solution)/shard_map/pallas_call | solution.py:326
